TPU v7x, 256 devices: a whole 4x4x8 slice. The times are simulated.
256 devices in a mesh: slab: 32 (over x, z), col: 4 (over y), pb: 2 (over core).
Axes of the slice: x: 4, y: 4, z: 8, core: 2. Of those that a mesh axis runs over, the one named last changes fastest.
Arguments:
- queries_raw: float32 [1024, 768], P(('slab', 'col', 'pb')), may hold values from -1.5 to 1.5
- projection: float32 [768, 768], replicated, may hold values from -0.21875 to 0.21875
- passages: bfloat16 [524288, 768], P(('slab', 'col')), may hold values from -17 to 17
- positives: int32 [1024, 4], P(('slab', 'col', 'pb')), may hold values from 0 to 524287
Outputs:
- loss: float32 [1024], P(('slab', 'col', 'pb'))
- grad_raw: float32 [1024, 768], P(('slab', 'col', 'pb'))
- grad_projection: float32 [768, 768], replicated
All inputs are finite; a program needn't handle non-finite values.
Results may differ from a plain program's by a relative error of at most 0.0053.
Values may be sent and summed in bfloat16 or wider, within the bound.
No kernel may reach another device: no remote copies, remote signals or barrier semaphores. Data moves between devices by JAX's collectives and lax.ppermute only.
A program may use at most 128 MiB of HBM per device.

v0:
```python
import jax
import jax.numpy as jnp
from jax import lax
from jax.sharding import PartitionSpec as P

POS = 4


def shards(queries_raw, projection, passages, positives):
    hp = lax.Precision.HIGHEST
    local_rows = passages.shape[0]
    own_queries = queries_raw.shape[0]
    group = lax.axis_size(("slab", "col"))
    scale = 1.0 / (4.0 * local_rows * group)
    projected = jnp.dot(queries_raw, projection, precision=hp, preferred_element_type=jnp.float32)
    query_emb = projected.astype(jnp.bfloat16)
    all_emb, all_pos = (
        lax.all_gather(query_emb, ("slab", "col"), axis=0, tiled=True),
        lax.all_gather(positives, ("slab", "col"), axis=0, tiled=True),
    )
    offset = lax.axis_index(("slab", "col")) * local_rows
    scores = lax.dot_general(
        all_emb, passages, (((1,), (1,)), ((), ())), preferred_element_type=jnp.float32
    )
    columns = jnp.arange(local_rows, dtype=jnp.int32)[None, :]
    local_pos = all_pos - offset
    owned = [local_pos[:, slot : slot + 1] == columns for slot in range(POS)]
    partial_pos = jnp.stack(
        [jnp.sum(jnp.where(owned[slot], scores, 0.0), axis=1) for slot in range(POS)], axis=1
    )
    pos_scores = lax.psum(partial_pos, ("slab", "col"))
    loss_part = jnp.zeros((scores.shape[0],), jnp.float32)
    slope_sum = jnp.zeros_like(scores)
    pos_list = []
    for slot in range(POS):
        sig = jax.nn.sigmoid(scores - pos_scores[:, slot : slot + 1])
        loss_part = loss_part + jnp.sum(sig, axis=1)
        slope = sig * (1.0 - sig)
        slope_sum = slope_sum + slope
        pos_list.append(-jnp.sum(slope, axis=1))
    pos_part = jnp.stack(pos_list, axis=1) * scale
    pos_grad, loss_total = lax.psum((pos_part, loss_part * scale), ("slab", "col"))
    grad = slope_sum * scale
    for slot in range(POS):
        grad = grad + jnp.where(owned[slot], pos_grad[:, slot : slot + 1], 0.0)
    grad_b = grad.astype(jnp.bfloat16)
    home = lax.axis_index(("slab", "col")) * own_queries
    summed = lax.psum(
        jnp.dot(grad_b, passages, preferred_element_type=jnp.float32), ("slab", "col")
    )
    query_grad = lax.dynamic_slice_in_dim(summed, home, own_queries, 0)
    loss = lax.dynamic_slice_in_dim(loss_total, home, own_queries, 0)
    grad_raw = jnp.dot(query_grad, projection.T, precision=hp, preferred_element_type=jnp.float32)
    term = jnp.dot(queries_raw.T, query_grad, precision=hp, preferred_element_type=jnp.float32)
    grad_projection = lax.psum(term, ("slab", "col", "pb"))
    return (loss, grad_raw, grad_projection)


def solution(mesh):
    in_specs = (
        P(("slab", "col", "pb"), None),
        P(),
        P(("slab", "col"), None),
        P(("slab", "col", "pb"), None),
    )
    out_specs = (P(("slab", "col", "pb")), P(("slab", "col", "pb"), None), P())
    return jax.shard_map(shards, mesh=mesh, in_specs=in_specs, out_specs=out_specs, check_vma=False)
```

profile of v0, /device:TPU:2, one launch (start us, length us, event | category | flops | bytes accessed | tf_op | source)
XLA Modules:
  0.0 2272.7 jit_solution(6751082720767750001)
XLA Ops:
  7.2 0.0 all-reduce.4.cloned.1.call-start
  7.2 309.0 %all-gather.1 = s32[128,4,4]{2,1,0:T(4,128)S(1)} all-gather(s32[1,4,4]{2,1,0:T(4,128)} %bitcast.45), channel_id=1, replica_groups=mesh['slab'=32,'col'=4,'pb'=2] {'slab','col'}, dimensions={0}, use_global_device_ids=true | all-gather | bytes 8256 | tf_op jit(solution)/shard_map/all_gather | solution.py:19
  316.2 1.9 fusion.5
  318.1 305.6 %all-gather = bf16[128,4,768]{2,1,0:T(4,128)(2,1)S(1)} all-gather(bf16[1,4,768]{2,1,0:T(4,128)(2,1)S(1)} %fusion.5), channel_id=1, replica_groups=mesh['slab'=32,'col'=4,'pb'=2] {'slab','col'}, dimensions={0}, use_global_device_ids=true | all-gather | bytes 792576 | tf_op jit(solution)/shard_map/all_gather | solution.py:18
  623.7 1.1 reshape.39
  624.8 0.3 fusion.14
  625.1 0.1 copy.19
  625.2 0.1 copy.20
  625.3 0.1 copy.18
  625.4 0.1 copy.21
  625.6 11.6 select_reduce_fusion.3
  637.2 348.3 %psum.35 = f32[512,4]{0,1:T(4,128)S(1)} all-reduce(f32[512,4]{0,1:T(4,128)S(1)} %pad_maximum_fusion), channel_id=1, replica_groups=mesh['slab'=32,'col'=4,'pb'=2] {'slab','col'}, use_global_device_ids=true, to_apply=%region_4.5 | all-reduce | flops 2048 | bytes 16384 | tf_op jit(solution)/shard_map/psum | solution.py:31
  985.5 17.1 fusion.1
  1002.7 681.8 %all-reduce = (f32[512]{0:T(512)S(1)}, f32[512,4]{0,1:T(4,128)S(1)}) all-reduce(f32[512]{0:T(512)S(1)} %add_multiply_fusion, f32[512,4]{0,1:T(4,128)S(1)} %maximum_multiply_fusion), channel_id=1, replica_groups=mesh['slab'=32,'col'=4,'pb'=2] {'slab','col'}, use_global_device_ids=true, to_apply=%region_9.10 | all-reduce | flops 2560 | bytes 20480 | tf_op jit(solution)/shard_map/psum | solution.py:42
  1684.5 21.1 fusion.4
  1705.6 0.0 all-reduce.4.cloned.1.call-update
  1705.7 0.0 all-reduce.6.cloned.1.call-start
  1705.7 291.5 %all-reduce.4.cloned.1.call-done = f32[512,768]{1,0:T(8,128)} async-done(((f32[512,768]{1,0:T(8,128)}), f32[512,768]{1,0:T(8,128)}) %all-reduce.4.cloned.1.call-update) | async-done | bytes 1572880 | tf_op jit(solution)/shard_map/psum | solution.py:48
  1997.2 4.2 convolution_bitcast_fusion
  2001.4 0.0 all-reduce.6.cloned.1.call-update
  2001.4 0.6 dynamic_slice.6
  2002.0 3.4 fusion.7
  2005.4 257.4 %all-reduce.6.cloned.1.call-done = f32[768,768]{0,1:T(8,128)} async-done(((f32[768,768]{0,1:T(8,128)}), f32[768,768]{0,1:T(8,128)}) %all-reduce.6.cloned.1.call-update) | async-done | bytes 2359312 | tf_op jit(solution)/shard_map/psum | solution.py:55
  2262.8 3.0 copy.17
  (14 shorter events, 0.1 us)
Async XLA Ops:
  7.2 309.0 %copy-start = (f32[768,768]{1,0:T(8,128)S(1)}, f32[768,768]{1,0:T(8,128)}, u32[]{:S(2)}) copy-start(f32[768,768]{1,0:T(8,128)} %param.5) | copy-start | bytes 7077892
  7.2 1990.0 %all-reduce.4.cloned.1.call-start = ((), (), s32[]{:S(2)}) async-start(), calls=%async_computation | async-start | bytes 3145728 | tf_op jit(solution)/shard_map/psum | solution.py:48
  1684.5 312.7 %copy-start.1 = (f32[4,768]{1,0:T(4,128)S(1)}, f32[4,768]{1,0:T(4,128)}, u32[]{:S(2)}) copy-start(f32[4,768]{1,0:T(4,128)} %param.4) | copy-start | bytes 36868
  1705.7 557.1 %all-reduce.6.cloned.1.call-start = ((), (), s32[]{:S(2)}) async-start(), calls=%async_computation.1 | async-start | bytes 4718592 | tf_op jit(solution)/shard_map/psum | solution.py:55
Sparse Core Ops, SparseCore 0:
  1705.8 291.3 all-reduce.3
  2004.1 258.6 all-reduce.5
where the time goes:
time: 2270 us
  blocking collectives  1640 us (72%)
  waiting for transfers between devices  549 us (24%)
  matrix products  42.2 us (2%)
    psum x1, blocking collectives, shards(): lax.psum((pos_part, loss_part * scale), ('slab', 'col'))  682 us
    psum x1, blocking collectives, shards(): pos_scores = lax.psum(partial_pos, ('slab', 'col'))  348 us
    all_gather x1, blocking collectives, shards(): lax.all_gather(positives, ('slab', 'col'), axis=0, tiled=True)  309 us
    all_gather x1, blocking collectives, shards(): lax.all_gather(query_emb, ('slab', 'col'), axis=0, tiled=True)  306 us
    psum x1, waiting for transfers between devices, shards(): lax.psum(jnp.dot(grad_b, passages, preferred_element_type=jnp.float32), (...  291 us
    psum x1, waiting for transfers between devices, shards(): grad_projection = lax.psum(term, ('slab', 'col', 'pb'))  257 us
  transfers between devices with their start and end apart: 2, of which 2 were waited for; matrix products, arithmetic and copies ran while one was open for 0% of the time, Pallas kernels for 0%

commit v1 on v0

--- a/solution.py
+++ b/solution.py
@@ -52,7 +52,7 @@
     loss = lax.dynamic_slice_in_dim(loss_total, home, own_queries, 0)
     grad_raw = jnp.dot(query_grad, projection.T, precision=hp, preferred_element_type=jnp.float32)
     term = jnp.dot(queries_raw.T, query_grad, precision=hp, preferred_element_type=jnp.float32)
-    grad_projection = lax.psum(term, ("slab", "col", "pb"))
+    grad_projection = lax.psum(lax.psum(term, "slab"), ("col", "pb"))
     return (loss, grad_raw, grad_projection)
 
 

time: 2270 us -> 2240 us (0.987)
  waiting for transfers between devices: 549 us -> 511 us
    psum x1 -> x2, waiting for transfers between devices: 257 us -> 220 us  [shards(): grad_projection = lax.psum(lax.psum(term, 'slab'), ('col', 'pb'))]
  transfers between devices with their start and end apart: 2 -> 3, of which waited for: 2 -> 3; matrix products, arithmetic and copies ran while one was open for 0% -> 0% of each run, Pallas kernels for 0% -> 0%
where the time goes in v1:
time: 2240 us; the launch traced here: 2230 us
  blocking collectives  1640 us (73%)
  waiting for transfers between devices  511 us (23%)
  matrix products  42.2 us (2%)
    psum x1, blocking collectives, shards(): lax.psum((pos_part, loss_part * scale), ('slab', 'col'))  682 us
    psum x1, blocking collectives, shards(): pos_scores = lax.psum(partial_pos, ('slab', 'col'))  348 us
    all_gather x1, blocking collectives, shards(): lax.all_gather(positives, ('slab', 'col'), axis=0, tiled=True)  309 us
    all_gather x1, blocking collectives, shards(): lax.all_gather(query_emb, ('slab', 'col'), axis=0, tiled=True)  306 us
    psum x1, waiting for transfers between devices, shards(): lax.psum(jnp.dot(grad_b, passages, preferred_element_type=jnp.float32), (...  291 us
    psum x2, waiting for transfers between devices, shards(): grad_projection = lax.psum(lax.psum(term, 'slab'), ('col', 'pb'))  220 us
  transfers between devices with their start and end apart: 3, of which 3 were waited for; matrix products, arithmetic and copies ran while one was open for 0% of the time, Pallas kernels for 0%

profile of v1, /device:TPU:2, one launch (start us, length us, event | category | flops | bytes accessed | tf_op | source)
XLA Modules:
  0.0 2234.9 jit_solution(16618343698675075239)
XLA Ops:
  7.2 0.0 all-reduce.5.cloned.1.call-start
  7.2 309.0 %all-gather.1 = s32[128,4,4]{2,1,0:T(4,128)S(1)} all-gather(s32[1,4,4]{2,1,0:T(4,128)} %bitcast.45), channel_id=1, replica_groups=mesh['slab'=32,'col'=4,'pb'=2] {'slab','col'}, dimensions={0}, use_global_device_ids=true | all-gather | bytes 8256 | tf_op jit(solution)/shard_map/all_gather | solution.py:19
  316.2 1.9 fusion.5
  318.1 305.6 %all-gather = bf16[128,4,768]{2,1,0:T(4,128)(2,1)S(1)} all-gather(bf16[1,4,768]{2,1,0:T(4,128)(2,1)S(1)} %fusion.5), channel_id=1, replica_groups=mesh['slab'=32,'col'=4,'pb'=2] {'slab','col'}, dimensions={0}, use_global_device_ids=true | all-gather | bytes 792576 | tf_op jit(solution)/shard_map/all_gather | solution.py:18
  623.7 1.1 reshape.39
  624.8 0.3 fusion.14
  625.1 0.1 copy.19
  625.2 0.1 copy.20
  625.3 0.1 copy.18
  625.4 0.1 copy.21
  625.6 11.6 select_reduce_fusion.3
  637.2 348.3 %psum.42 = f32[512,4]{0,1:T(4,128)S(1)} all-reduce(f32[512,4]{0,1:T(4,128)S(1)} %pad_maximum_fusion), channel_id=1, replica_groups=mesh['slab'=32,'col'=4,'pb'=2] {'slab','col'}, use_global_device_ids=true, to_apply=%region_4.5 | all-reduce | flops 2048 | bytes 16384 | tf_op jit(solution)/shard_map/psum | solution.py:31
  985.5 17.1 fusion.1
  1002.7 681.8 %all-reduce = (f32[512]{0:T(512)S(1)}, f32[512,4]{0,1:T(4,128)S(1)}) all-reduce(f32[512]{0:T(512)S(1)} %add_multiply_fusion, f32[512,4]{0,1:T(4,128)S(1)} %maximum_multiply_fusion), channel_id=1, replica_groups=mesh['slab'=32,'col'=4,'pb'=2] {'slab','col'}, use_global_device_ids=true, to_apply=%region_9.10 | all-reduce | flops 2560 | bytes 20480 | tf_op jit(solution)/shard_map/psum | solution.py:42
  1684.5 21.1 fusion.4
  1705.7 0.0 all-reduce.7.cloned.1.call-start
  1705.7 291.5 %all-reduce.5.cloned.1.call-done = f32[512,768]{1,0:T(8,128)} async-done(((f32[512,768]{1,0:T(8,128)}), f32[512,768]{1,0:T(8,128)}) %all-reduce.5.cloned.1.call-update) | async-done | bytes 1572880 | tf_op jit(solution)/shard_map/psum | solution.py:48
  1997.2 4.2 convolution_bitcast_fusion
  2001.4 0.0 all-reduce.9.cloned.1.call-start
  2001.5 151.1 %all-reduce.7.cloned.1.call-done = f32[768,768]{0,1:T(8,128)} async-done(((f32[768,768]{0,1:T(8,128)}), f32[768,768]{0,1:T(8,128)}) %all-reduce.7.cloned.1.call-update) | async-done | bytes 2359312 | tf_op jit(solution)/shard_map/psum | solution.py:55
  2152.6 0.6 dynamic_slice.6
  2153.2 3.4 fusion.7
  2156.5 68.8 %all-reduce.9.cloned.1.call-done = f32[768,768]{0,1:T(8,128)} async-done(((f32[768,768]{0,1:T(8,128)}), f32[768,768]{0,1:T(8,128)}) %all-reduce.9.cloned.1.call-update) | async-done | bytes 2359312 | tf_op jit(solution)/shard_map/psum | solution.py:55
  2225.3 3.0 copy.17
  (17 shorter events, 0.2 us)
Async XLA Ops:
  7.2 309.0 %copy-start = (f32[768,768]{1,0:T(8,128)S(1)}, f32[768,768]{1,0:T(8,128)}, u32[]{:S(2)}) copy-start(f32[768,768]{1,0:T(8,128)} %param.5) | copy-start | bytes 7077892
  7.2 1990.0 %all-reduce.5.cloned.1.call-start = ((), (), s32[]{:S(2)}) async-start(), calls=%async_computation | async-start | bytes 3145728 | tf_op jit(solution)/shard_map/psum | solution.py:48
  1684.5 312.7 %copy-start.1 = (f32[4,768]{1,0:T(4,128)S(1)}, f32[4,768]{1,0:T(4,128)}, u32[]{:S(2)}) copy-start(f32[4,768]{1,0:T(4,128)} %param.4) | copy-start | bytes 36868
  1705.7 446.9 %all-reduce.7.cloned.1.call-start = ((), (), s32[]{:S(2)}) async-start(), calls=%async_computation.1 | async-start | bytes 4718592 | tf_op jit(solution)/shard_map/psum | solution.py:55
  2001.4 223.9 %all-reduce.9.cloned.1.call-start = ((), (), s32[]{:S(2)}) async-start(), calls=%async_computation.2 | async-start | bytes 4718592 | tf_op jit(solution)/shard_map/psum | solution.py:55
Sparse Core Ops, SparseCore 0:
  1705.8 291.3 all-reduce.4
  2001.7 150.7 all-reduce.6
  2154.9 70.3 all-reduce.8

commit v2 on v0

--- a/solution.py
+++ b/solution.py
@@ -39,7 +39,7 @@
         slope_sum = slope_sum + slope
         pos_list.append(-jnp.sum(slope, axis=1))
     pos_part = jnp.stack(pos_list, axis=1) * scale
-    pos_grad, loss_total = lax.psum((pos_part, loss_part * scale), ("slab", "col"))
+    pos_grad, loss_total = lax.psum(lax.psum((pos_part, loss_part * scale), "col"), "slab")
     grad = slope_sum * scale
     for slot in range(POS):
         grad = grad + jnp.where(owned[slot], pos_grad[:, slot : slot + 1], 0.0)

time: 2270 us -> 1740 us (0.77)
  blocking collectives: 1640 us -> 1180 us
  waiting for transfers between devices: 549 us -> 485 us
    psum x1 -> x2, blocking collectives: 682 us -> 218 us  [the longest x1 203 us: shards(): lax.psum(lax.psum((pos_part, loss_part * scale), 'col'), 'slab')]
    psum x1, waiting for transfers between devices: 291 us -> 227 us  [shards(): lax.psum(jnp.dot(grad_b, passages, preferred_element_type=jnp.float32), (...]
where the time goes in v2:
time: 1740 us
  blocking collectives  1180 us (68%)
  waiting for transfers between devices  485 us (28%)
  matrix products  42.2 us (2%)
    psum x1, blocking collectives, shards(): pos_scores = lax.psum(partial_pos, ('slab', 'col'))  348 us
    all_gather x1, blocking collectives, shards(): lax.all_gather(positives, ('slab', 'col'), axis=0, tiled=True)  309 us
    all_gather x1, blocking collectives, shards(): lax.all_gather(query_emb, ('slab', 'col'), axis=0, tiled=True)  306 us
    psum x1, waiting for transfers between devices, shards(): grad_projection = lax.psum(term, ('slab', 'col', 'pb'))  257 us
    psum x1, waiting for transfers between devices, shards(): lax.psum(jnp.dot(grad_b, passages, preferred_element_type=jnp.float32), (...  227 us
    psum x1, blocking collectives, shards(): lax.psum(lax.psum((pos_part, loss_part * scale), 'col'), 'slab')  203 us
  transfers between devices with their start and end apart: 2, of which 2 were waited for; matrix products, arithmetic and copies ran while one was open for 0% of the time, Pallas kernels for 0%

profile of v2, /device:TPU:2, one launch (start us, length us, event | category | flops | bytes accessed | tf_op | source)
XLA Modules:
  0.0 1744.2 jit_solution(11891850312172584024)
XLA Ops:
  7.2 0.0 all-reduce.5.cloned.1.call-start
  7.2 309.0 %all-gather.1 = s32[128,4,4]{2,1,0:T(4,128)S(1)} all-gather(s32[1,4,4]{2,1,0:T(4,128)} %bitcast.45), channel_id=1, replica_groups=mesh['slab'=32,'col'=4,'pb'=2] {'slab','col'}, dimensions={0}, use_global_device_ids=true | all-gather | bytes 8256 | tf_op jit(solution)/shard_map/all_gather | solution.py:19
  316.2 1.9 fusion.5
  318.1 305.6 %all-gather = bf16[128,4,768]{2,1,0:T(4,128)(2,1)S(1)} all-gather(bf16[1,4,768]{2,1,0:T(4,128)(2,1)S(1)} %fusion.5), channel_id=1, replica_groups=mesh['slab'=32,'col'=4,'pb'=2] {'slab','col'}, dimensions={0}, use_global_device_ids=true | all-gather | bytes 792576 | tf_op jit(solution)/shard_map/all_gather | solution.py:18
  623.7 1.1 reshape.39
  624.8 0.3 fusion.14
  625.1 0.1 copy.19
  625.2 0.1 copy.20
  625.3 0.1 copy.18
  625.4 0.1 copy.21
  625.6 11.6 select_reduce_fusion.3
  637.2 348.3 %psum.49 = f32[512,4]{0,1:T(4,128)S(1)} all-reduce(f32[512,4]{0,1:T(4,128)S(1)} %pad_maximum_fusion), channel_id=1, replica_groups=mesh['slab'=32,'col'=4,'pb'=2] {'slab','col'}, use_global_device_ids=true, to_apply=%region_4.5 | all-reduce | flops 2048 | bytes 16384 | tf_op jit(solution)/shard_map/psum | solution.py:31
  985.5 17.1 fusion.1
  1002.7 14.3 all-reduce.1
  1017.0 203.3 %all-reduce = (f32[512]{0:T(512)S(1)}, f32[512,4]{0,1:T(4,128)S(1)}) all-reduce(f32[512]{0:T(512)S(1)} %get-tuple-element.26, f32[512,4]{0,1:T(4,128)S(1)} %get-tuple-element.27), channel_id=1, replica_groups=mesh['slab'=32,'col'=4,'pb'=2] {'slab'}, use_global_device_ids=true, to_apply=%region_10.11 | all-reduce | flops 2560 | bytes 20480 | tf_op jit(solution)/shard_map/psum | solution.py:42
  1220.4 21.1 %fusion.4 = f32[512,768]{1,0:T(8,128)} fusion(bf16[4096,768]{1,0:T(8,128)(2,1)} %param.6, f32[512,4096]{1,0:T(8,128)} %get-tuple-element.34, f32[512,4096]{1,0:T(8,128)} %get-tuple-element.28, f32[512,4096]{1,0:T(8,128)} %get-tuple-element.40, f32[512,4096]{1,0:T(8,128)} %get-tuple-element.37, f32[512]{0:T(512)S(1)} %bitcast.55, f32[512]{0:T(512)S(1)} %bitcast.56, ...), kind=kOutput, calls=%fused_computation.21 | convolution fusion | flops 3273654272 | bytes 41435136 | tf_op jit(solution)/shard_map/dot_general | solution.py:49
  1241.4 0.0 all-reduce.5.cloned.1.call-update
  1241.5 0.0 all-reduce.7.cloned.1.call-start
  1241.5 227.2 %all-reduce.5.cloned.1.call-done = f32[512,768]{1,0:T(8,128)} async-done(((f32[512,768]{1,0:T(8,128)}), f32[512,768]{1,0:T(8,128)}) %all-reduce.5.cloned.1.call-update) | async-done | bytes 1572880 | tf_op jit(solution)/shard_map/psum | solution.py:48
  1468.7 4.2 convolution_bitcast_fusion
  1472.9 0.6 dynamic_slice.6
  1473.5 3.4 fusion.7
  1476.9 257.4 %all-reduce.7.cloned.1.call-done = f32[768,768]{0,1:T(8,128)} async-done(((f32[768,768]{0,1:T(8,128)}), f32[768,768]{0,1:T(8,128)}) %all-reduce.7.cloned.1.call-update) | async-done | bytes 2359312 | tf_op jit(solution)/shard_map/psum | solution.py:55
  1734.3 3.0 copy.17
  (15 shorter events, 0.1 us)
Async XLA Ops:
  7.2 309.0 %copy-start = (f32[768,768]{1,0:T(8,128)S(1)}, f32[768,768]{1,0:T(8,128)}, u32[]{:S(2)}) copy-start(f32[768,768]{1,0:T(8,128)} %param.5) | copy-start | bytes 7077892
  7.2 1461.5 %all-reduce.5.cloned.1.call-start = ((), (), s32[]{:S(2)}) async-start(), calls=%async_computation | async-start | bytes 3145728 | tf_op jit(solution)/shard_map/psum | solution.py:48
  1220.3 248.4 %copy-start.1 = (f32[4,768]{1,0:T(4,128)S(1)}, f32[4,768]{1,0:T(4,128)}, u32[]{:S(2)}) copy-start(f32[4,768]{1,0:T(4,128)} %param.4) | copy-start | bytes 36868
  1241.5 492.8 %all-reduce.7.cloned.1.call-start = ((), (), s32[]{:S(2)}) async-start(), calls=%async_computation.1 | async-start | bytes 4718592 | tf_op jit(solution)/shard_map/psum | solution.py:55
Sparse Core Ops, SparseCore 0:
  1241.6 227.0 all-reduce.4
  1475.6 258.6 all-reduce.6
